TPU v7x, 256 devices: a whole 4x4x8 slice. The times are simulated.
256 devices in a mesh: dp: 8 (over z), cls: 32 (over y, x, core).
Axes of the slice: x: 4, y: 4, z: 8, core: 2. Of those that a mesh axis runs over, the one named last changes fastest.
Arguments:
- weak_embed: bfloat16 [512, 512], P('dp'), may hold values from -6 to 6
- strong_embed: bfloat16 [512, 512], P('dp'), may hold values from -0.0625 to 0.0625
- centers: bfloat16 [1048576, 512], P(('dp', 'cls')), may hold values from -0.0625 to 0.0625
- marginal: float32 [1048576], P(('dp', 'cls')), may hold values from 0.25 to 45
- pseudo_label: int32 [512], P('dp'), may hold values from 0 to 1048575
- confident: int32 [512], P('dp'), may hold values 0 or 1
Outputs:
- new_marginal: float32 [1048576], P(('dp', 'cls'))
- center_grad: bfloat16 [1048576, 512], P(('dp', 'cls'))
- embed_grad: float32 [512, 512], P('dp')
- loss: float32 [], replicated
All inputs are finite; a program needn't handle non-finite values. No bound on the sum of `confident` on one device may be relied on, other than what follows from the above.
Results may differ from a plain program's by a relative error of at most 0.00155.
The roundings to bfloat16 on the way count: a program that leaves them out, or rounds other values in their place, can miss the bound.
Values may be sent and summed in bfloat16 or wider, within the bound.
A program may use at most 128 MiB of HBM per device.

v0:
```python
import jax
import jax.numpy as jnp
from jax import lax
from jax.sharding import PartitionSpec as P

SCALE = 64.0
MARGIN = 0.35
MOMENTUM = 0.9
EPS = 1e-06


def unit_rows(values):
    exact = values.astype(jnp.float32)
    inverse = lax.rsqrt(jnp.sum(exact * exact, axis=-1, keepdims=True) + EPS)
    return (exact * inverse, inverse)


def body(weak_embed, strong_embed, centers, marginal, pseudo_label, confident):
    img = strong_embed.shape[0]
    cls_dev = centers.shape[0]
    weak_exact, _ = unit_rows(weak_embed)
    strong_exact, strong_inv = unit_rows(strong_embed)
    stacked = jnp.stack([weak_exact.astype(jnp.bfloat16), strong_exact.astype(jnp.bfloat16)])
    views, labels, flag_ints = (
        lax.all_gather(stacked, "dp", axis=1, tiled=True),
        lax.all_gather(pseudo_label, "dp", axis=0, tiled=True),
        lax.all_gather(confident, "dp", axis=0, tiled=True),
    )
    row_count = views.shape[1]
    width = views.shape[2]
    flags = flag_ints.astype(jnp.float32)
    center_exact, center_inv = unit_rows(centers)
    center_unit = center_exact.astype(jnp.bfloat16)
    scores = lax.dot_general(
        views.reshape(2 * row_count, width),
        center_unit,
        (((1,), (1,)), ((), ())),
        preferred_element_type=jnp.float32,
    )
    teach = jnp.exp(SCALE * (scores[:row_count] - 1.0))
    offset = (lax.axis_index("dp") * lax.axis_size("cls") + lax.axis_index("cls")) * cls_dev
    ids = offset + jnp.arange(cls_dev, dtype=jnp.int32)
    hit = (labels[:, None] == ids[None, :]).astype(jnp.float32)
    stud = SCALE * (scores[row_count:] - MARGIN * hit)
    teach_part = jnp.sum(teach, axis=1)
    stud_part = jnp.sum(jnp.exp(stud - SCALE), axis=1)
    label_part = jnp.sum(hit * stud, axis=1)
    classes_total = cls_dev * lax.axis_size("dp") * lax.axis_size("cls")
    teacher_total = lax.psum(teach_part, ("dp", "cls"))
    share = teach / teacher_total[:, None]
    batch = classes_total / row_count * jnp.sum(share, axis=0)
    fresh = MOMENTUM * marginal + (1.0 - MOMENTUM) * batch
    raw = share / fresh[None, :]
    fresh, raw, q_part, r_part = (fresh, raw, jnp.sum(raw, axis=1), jnp.sum(raw * stud, axis=1))
    aligned_total, aligned_cross = lax.psum((q_part, r_part), ("dp", "cls"))
    student_total, label_logit = lax.psum((stud_part, label_part), ("dp", "cls"))
    loss = (
        jnp.sum(
            flags
            * (
                SCALE
                + jnp.log(student_total)
                - 0.5 * label_logit
                - 0.5 * aligned_cross / aligned_total
            )
        )
        / img
    )
    grad = (
        SCALE
        / img
        * flags[:, None]
        * (
            jnp.exp(stud - SCALE) / student_total[:, None]
            - 0.5 * hit
            - 0.5 * raw / aligned_total[:, None]
        )
    )
    grad = grad.astype(jnp.bfloat16)
    unit_part = jnp.dot(grad, center_unit, preferred_element_type=jnp.float32)
    unit_total = lax.psum(unit_part, ("dp", "cls"))
    unit_grad = lax.dynamic_slice_in_dim(unit_total, lax.axis_index("dp") * img, img, 0)
    embed_grad = (
        unit_grad - strong_exact * jnp.sum(strong_exact * unit_grad, axis=1, keepdims=True)
    ) * strong_inv
    cgrad = lax.dot_general(
        grad, views[1], (((0,), (0,)), ((), ())), preferred_element_type=jnp.float32
    )
    cgrad = (
        cgrad - center_exact * jnp.sum(center_exact * cgrad, axis=1, keepdims=True)
    ) * center_inv
    return (fresh, cgrad.astype(jnp.bfloat16), embed_grad, loss)


def solution(mesh):
    placed = (
        P("dp", None),
        P("dp", None),
        P(("dp", "cls"), None),
        P(("dp", "cls")),
        P("dp"),
        P("dp"),
    )
    return jax.shard_map(
        body,
        mesh=mesh,
        in_specs=placed,
        out_specs=(P(("dp", "cls")), P(("dp", "cls"), None), P("dp", None), P()),
        check_vma=False,
    )
```

profile of v0, /device:TPU:1, one launch (start us, length us, event | category | flops | bytes accessed | tf_op | source)
XLA Modules:
  0.0 507.4 jit_solution(5591353796502979499)
XLA Ops:
  7.2 0.0 copy-start.10
  7.2 0.0 copy-start.8
  7.2 0.0 copy-start.9
  7.2 0.0 all-gather.2.cloned.1.call-start
  7.2 1.0 fusion.32
  8.2 1.0 fusion.27
  9.2 1.0 fusion.33
  10.2 0.7 pad_maximum_fusion
  10.8 0.0 all-gather.2.cloned.1.call-update
  10.9 0.0 all-reduce.6.cloned.1.call-start
  10.9 6.3 %copy.10 = bf16[4096,512]{0,1:T(8,128)(2,1)} copy(bf16[4096,512]{1,0:T(8,128)(2,1)} %param.8) | data formatting | bytes 8388608 | tf_op args[2]
  17.2 0.0 copy-done.10
  17.2 0.6 dynamic-slice
  18.5 0.0 copy-done.8
  18.5 0.2 dynamic-update-slice
  18.7 0.0 copy-done.9
  18.7 0.2 dynamic-update-slice.1
  19.0 14.1 %all-reduce.2 = (s32[512]{0:T(512)S(1)}, s32[512]{0:T(512)S(1)}) all-reduce(s32[512]{0:T(512)S(1)} %dynamic-update-slice.1, s32[512]{0:T(512)S(1)} %dynamic-update-slice), channel_id=1, replica_groups=mesh['dp'=8,'cls'=32] {'dp'}, use_global_device_ids=true, to_apply=%add.1 | all-reduce | flops 1024 | bytes 8192
  33.0 3.1 fusion.7
  36.1 12.3 %all-gather.2.cloned.1.call-done = bf16[2,512,512]{2,1,0:T(8,128)(2,1)} async-done(((bf16[2,64,512]{2,1,0:T(8,128)(2,1)}), bf16[2,512,512]{2,1,0:T(8,128)(2,1)}) %all-gather.2.cloned.1.call-update) | async-done | bytes 1048592 | tf_op jit(solution)/shard_map/all_gather | solution.py:25
  48.4 6.6 %fusion.21 = f32[1024,4096]{1,0:T(8,128)S(1)} fusion(bf16[1024,512]{1,0:T(8,128)(2,1)} %bitcast.14, bf16[4096,512]{0,1:T(8,128)(2,1)} %copy.10, f32[4096]{0:T(1024)S(1)} %add_rsqrt_fusion), kind=kOutput, calls=%fused_computation.30 | convolution fusion | flops 4301258752 | bytes 22036480 | tf_op jit(solution)/shard_map/dot_general | solution.py:34
  55.0 0.0 copy-start
  55.0 5.7 %copy-done = f32[1024,4096]{1,0:T(8,128)} copy-done((f32[1024,4096]{1,0:T(8,128)}, f32[1024,4096]{1,0:T(8,128)S(1)}, u32[]{:S(2)}) %copy-start) | copy-done | bytes 16777240
  60.7 1.5 fusion.18
  62.3 79.6 %psum.42 = f32[512]{0:T(512)S(1)} all-reduce(f32[512]{0:T(512)S(1)} %fusion.18), channel_id=1, replica_groups=mesh['dp'=8,'cls'=32] {'dp','cls'}, use_global_device_ids=true, to_apply=%region_4.0 | all-reduce | flops 512 | bytes 4096 | tf_op jit(solution)/shard_map/psum | solution.py:49
  141.9 4.4 divide_reduce_fusion
  146.3 0.0 copy-done.6
  146.3 0.0 copy-start.5
  146.3 10.2 %fusion.14 = (f32[512]{0:T(512)S(1)}, f32[512]{0:T(512)S(1)}, f32[512]{0:T(512)S(1)}, f32[512]{0:T(512)S(1)}) fusion(s32[4096]{0:T(1024)S(1)} %iota_add_fusion, s32[512]{0:T(512)S(1)} %get-tuple-element.12, f32[1024,4096]{1,0:T(8,128)} %copy-done, f32[4096]{0:T(1024)S(1)} %multiply_add_fusion, f32[512]{0:T(512)S(1)} %psum.42), kind=kLoop, calls=%fused_computation.19 | loop fusion | flops 31455232 | bytes 16822272 | tf_op jit(solution)/shard_map/reduce_sum | solution.py:47
  156.5 73.8 %all-reduce.3 = (f32[512]{0:T(512)S(1)}, f32[512]{0:T(512)S(1)}, f32[512]{0:T(512)S(1)}, f32[512]{0:T(512)S(1)}) all-reduce(f32[512]{0:T(512)S(1)} %get-tuple-element.10, f32[512]{0:T(512)S(1)} %get-tuple-element.11, f32[512]{0:T(512)S(1)} %get-tuple-element.9, f32[512]{0:T(512)S(1)} %get-tuple-element.8), channel_id=1, replica_groups=mesh['dp'=8,'cls'=32] {'dp','cls'}, use_global_device_ids=true, to_apply=%region_9.0 | all-reduce | flops 2048 | bytes 16384 | tf_op jit(solution)/shard_map/psum | solution.py:55
  230.4 0.0 copy-done.5
  230.4 9.6 %fusion.13 = bf16[512,4096]{1,0:T(8,128)(2,1)S(1)} fusion(f32[512]{0:T(512)S(1)} %get-tuple-element.14, f32[512]{0:T(512)S(1)} %get-tuple-element.15, s32[4096]{0:T(1024)S(1)} %iota_add_fusion, f32[512]{0:T(512)S(1)} %convert_element_type.34, s32[512]{0:T(512)S(1)} %get-tuple-element.12, f32[1024,4096]{1,0:T(8,128)} %copy-done, ...), kind=kLoop, calls=%fused_computation.18 | loop fusion | flops 35651584 | bytes 21014528 | tf_op jit(solution)/shard_map/convert_element_type | solution.py:79
  240.0 0.0 copy-start.3
  240.0 1.9 copy-done.3
  241.9 0.0 copy-done.1
  241.9 3.4 fusion.19
  245.3 0.0 all-reduce.6.cloned.1.call-update
  245.3 0.0 copy-done.7
  245.4 0.0 copy-start.2
  245.4 6.4 %fusion.3 = (f32[4096]{0:T(1024)S(1)}, f32[4096,512]{0,1:T(8,128)S(1)}) fusion(bf16[4096,512]{0,1:T(8,128)(2,1)} %copy.10, f32[4096]{0:T(1024)S(1)} %add_rsqrt_fusion, bf16[512,4096]{1,0:T(8,128)(2,1)} %copy-done.3, bf16[2,512,512]{2,1,0:T(8,128)(2,1)S(1)} %copy-done.7), kind=kOutput, calls=%fused_computation.8 | convolution fusion | flops 2155868160 | bytes 17334272 | tf_op jit(solution)/shard_map/dot_general | solution.py:86
  251.8 0.0 copy-done.2
  251.8 3.5 fusion.6
  255.3 6.4 %copy.11 = bf16[4096,512]{1,0:T(8,128)(2,1)} copy(bf16[4096,512]{0,1:T(8,128)(2,1)} %fusion.6) | data formatting | bytes 8388608
  261.8 0.6 multiply_reduce_fusion.1
  263.0 233.7 %all-reduce.6.cloned.1.call-done = f32[512,512]{1,0:T(8,128)} async-done(((f32[512,512]{1,0:T(8,128)}), f32[512,512]{1,0:T(8,128)}) %all-reduce.6.cloned.1.call-update) | async-done | bytes 1048592 | tf_op jit(solution)/shard_map/psum | solution.py:81
  496.7 0.0 copy-done.4
  496.7 1.1 fusion.29
  497.8 1.7 fusion.31
  (12 shorter events, 0.0 us)
Async XLA Ops:
  7.2 10.1 %copy-start.10 = (u32[256]{0:T(256)S(1)}, u32[256]{0:T(256)}, u32[]{:S(2)}) copy-start(u32[256]{0:T(256)} %constant.51) | copy-start | bytes 3076
  7.2 11.3 %copy-start.8 = (s32[64]{0:T(128)S(1)}, s32[64]{0:T(128)}, u32[]{:S(2)}) copy-start(s32[64]{0:T(128)} %param.11) | copy-start | bytes 772
  7.2 11.6 %copy-start.9 = (s32[64]{0:T(128)S(1)}, s32[64]{0:T(128)}, u32[]{:S(2)}) copy-start(s32[64]{0:T(128)} %param.10) | copy-start | bytes 772
  7.2 41.2 %all-gather.2.cloned.1.call-start = ((), (), s32[]{:S(2)}) async-start(), calls=%async_computation | async-start | bytes 1179648 | tf_op jit(solution)/shard_map/all_gather | solution.py:25
  10.9 485.8 %all-reduce.6.cloned.1.call-start = ((), (), s32[]{:S(2)}) async-start(), calls=%async_computation.1 | async-start | bytes 2097152 | tf_op jit(solution)/shard_map/psum | solution.py:81
  55.0 5.7 %copy-start = (f32[1024,4096]{1,0:T(8,128)}, f32[1024,4096]{1,0:T(8,128)S(1)}, u32[]{:S(2)}) copy-start(f32[1024,4096]{1,0:T(8,128)S(1)} %fusion.21) | copy-start | bytes 50331652
  60.7 85.5 %copy-start.6 = (f32[4096]{0:T(1024)S(1)}, f32[4096]{0:T(1024)}, u32[]{:S(2)}) copy-start(f32[4096]{0:T(1024)} %param.9) | copy-start | bytes 49156
  146.3 84.1 %copy-start.5 = (f32[4096]{0:T(1024)}, f32[4096]{0:T(1024)S(1)}, u32[]{:S(2)}) copy-start(f32[4096]{0:T(1024)S(1)} %multiply_add_fusion) | copy-start | bytes 49156
  230.4 11.6 %copy-start.1 = (bf16[4096,512]{0,1:T(8,128)(2,1)S(1)}, bf16[4096,512]{0,1:T(8,128)(2,1)}, u32[]{:S(2)}) copy-start(bf16[4096,512]{0,1:T(8,128)(2,1)} %copy.10) | copy-start | bytes 12582916
  240.0 1.9 copy-start.3
  241.9 3.4 copy-start.7
  245.4 6.5 %copy-start.2 = (bf16[4096,512]{0,1:T(8,128)(2,1)S(1)}, bf16[4096,512]{0,1:T(8,128)(2,1)}, u32[]{:S(2)}) copy-start(bf16[4096,512]{0,1:T(8,128)(2,1)} %copy.10) | copy-start | bytes 12582916
  255.3 241.4 %copy-start.4 = (bf16[64,512]{1,0:T(8,128)(2,1)S(1)}, bf16[64,512]{1,0:T(8,128)(2,1)}, u32[]{:S(2)}) copy-start(bf16[64,512]{1,0:T(8,128)(2,1)} %param.7) | copy-start | bytes 196612
Sparse Core Ops, SparseCore 0:
  11.0 37.3 all-gather.1
  245.5 251.1 all-reduce.5
where the time goes:
time: 509 us; the launch traced here: 507 us
  waiting for transfers between devices  246 us (48%)
  blocking collectives  168 us (33%)
  other arithmetic  39.3 us (8%)
  local copies, waits for them, and re-layouts  21.5 us (4%)
  between operations  16.7 us (3%)
  matrix products  16.4 us (3%)
    psum x1, waiting for transfers between devices, body(): unit_total = lax.psum(unit_part, ('dp', 'cls'))  234 us
    psum x1, blocking collectives, body(): teacher_total = lax.psum(teach_part, ('dp', 'cls'))  79.6 us
    psum x1, blocking collectives, body(): aligned_total, aligned_cross = lax.psum((q_part, r_part), ('dp', 'cls'))  73.8 us
    unnamed x29, local copies, waits for them, and re-layouts  21.5 us
    unnamed x1, blocking collectives  14.1 us
    all_gather x1, waiting for transfers between devices, body(): lax.all_gather(stacked, 'dp', axis=1, tiled=True)  12.3 us
    reduce_sum x1, other arithmetic, body(): label_part = jnp.sum(hit * stud, axis=1)  10.2 us
  transfers between devices with their start and end apart: 2, of which 2 were waited for; matrix products, arithmetic and copies ran while one was open for 5% of the time, Pallas kernels for 0%

commit v1 on v0

v1 whole, which is shorter than its diff:
```python
import functools
import math

import jax
import jax.numpy as jnp
from jax import lax
from jax.experimental import pallas as pl
from jax.experimental.pallas import tpu as pltpu
from jax.sharding import PartitionSpec as P

SCALE = 64.0
MARGIN = 0.35
MOMENTUM = 0.9
EPS = 1e-06
LOG2 = SCALE * math.log2(math.e)
MESH = pl.DeviceIdType.MESH
F32 = jnp.float32
BF16 = jnp.bfloat16
CH = 256
LANES = 128


def unit_rows(values):
    exact = values.astype(F32)
    inverse = lax.rsqrt(jnp.sum(exact * exact, axis=-1, keepdims=True) + EPS)
    return exact * inverse, inverse


def nt(a, b):
    return lax.dot_general(a, b, (((1,), (1,)), ((), ())), preferred_element_type=F32)


def kernel(
    nz, ncls,
    weak_hbm, strong_hbm, centers_hbm, marginal_hbm, label_hbm, flag_hbm,
    fresh_out, cgrad_out, egrad_out, loss_out,
    weak_own, strong_own, ints_own, marg,
    weak_all, strong_all, ints_all, label_row, flag_row,
    c_raw, c_unit, c_unit_t, c_inv, marg_col,
    teach, stud_dot, stud_exp, grad_t,
    vec_t, vec_q, vec_e,
    msg_a, msg_b, got_a, got_b,
    part_l, part_r, half_buf, half_got, plane_got, z_send, z_got, tile_own, tile_got,
    in_sem, c_sem,
    ring_send, ring_recv, sib_send, sib_recv, int_send, int_recv,
    a_send, a_recv, b_send, b_recv,
    half_send, half_recv, plane_send, plane_recv, z_send_sem, z_recv_sem, tile_send, tile_recv,
):
    img = weak_own.shape[0]
    half = img // 2
    classes = c_raw.shape[0]
    rows = weak_all.shape[0]
    width = weak_all.shape[1]
    blocks = rows // LANES
    nplane = ncls // 2
    z = lax.axis_index("dp")
    cls = lax.axis_index("cls")
    core = lax.rem(cls, 2)
    plane = lax.div(cls, 2)
    sibling = cls + 1 - 2 * core

    quarter = classes // 4
    own_copies = [
        pltpu.make_async_copy(weak_hbm, weak_own, in_sem.at[0]),
        pltpu.make_async_copy(strong_hbm, strong_own, in_sem.at[1]),
        pltpu.make_async_copy(label_hbm, ints_own.at[pl.ds(0, 1)], in_sem.at[2]),
        pltpu.make_async_copy(flag_hbm, ints_own.at[pl.ds(1, 1)], in_sem.at[3]),
        pltpu.make_async_copy(marginal_hbm, marg, in_sem.at[4]),
    ]
    for copy in own_copies:
        copy.start()
    c_copies = [
        pltpu.make_async_copy(
            centers_hbm.at[pl.ds(q * quarter, quarter)], c_raw.at[pl.ds(q * quarter, quarter)], c_sem.at[q]
        )
        for q in range(4)
    ]
    for copy in c_copies:
        copy.start()

    barrier = pltpu.get_barrier_semaphore()

    def greet_z(k, carry):
        pl.semaphore_signal(barrier, inc=1, device_id={"dp": lax.rem(z + k, nz)}, device_id_type=MESH)
        return carry

    def greet_cls(k, carry):
        pl.semaphore_signal(barrier, inc=1, device_id={"cls": lax.rem(cls + k, ncls)}, device_id_type=MESH)
        return carry

    lax.fori_loop(1, nz, greet_z, 0)
    lax.fori_loop(1, ncls, greet_cls, 0)

    own_copies[0].wait()
    own_copies[1].wait()
    base = pl.multiple_of(z * img, img)
    weak_exact, _ = unit_rows(weak_own[...])
    weak_all[pl.ds(base, img), :] = weak_exact.astype(BF16)
    strong_exact, strong_inv = unit_rows(strong_own[...])
    strong_all[pl.ds(base, img), :] = strong_exact.astype(BF16)
    own_copies[2].wait()
    own_copies[3].wait()
    mine = ints_own[:, 0:img]
    both = jnp.concatenate([mine, mine], axis=1)
    lane = lax.broadcasted_iota(jnp.int32, both.shape, 1)
    ints_all[z] = jnp.where(lax.div(lane, img) == lax.rem(z, 2), both, 0)

    pl.semaphore_wait(barrier, nz - 1 + ncls - 1)

    views = (weak_all, strong_all)
    hops = [(nz // 2, nz - 1 - nz // 2), (nz - 1 - nz // 2, nz // 2)]

    def piece(view, block):
        return views[view].at[pl.ds(pl.multiple_of(block * img + core * half, half), half)]

    def ring_copy(view, way, step):
        block = lax.rem(z - step + nz, nz) if way == 0 else lax.rem(z + step, nz)
        to = lax.rem(z + 1, nz) if way == 0 else lax.rem(z + nz - 1, nz)
        ref = piece(view, block)
        return pltpu.make_async_remote_copy(
            ref, ref, ring_send.at[view, way, step], ring_recv.at[view, way, step],
            device_id={"dp": to}, device_id_type=MESH,
        )

    def sib_copy(view, block):
        ref = piece(view, block)
        return pltpu.make_async_remote_copy(
            ref, ref, sib_send.at[view], sib_recv.at[view], device_id={"cls": sibling}, device_id_type=MESH
        )

    for view in range(2):
        for way in range(2):
            ring_copy(view, way, 0).start()

    def int_copy(k, carry):
        pltpu.make_async_remote_copy(
            ints_all.at[z], ints_all.at[z], int_send, int_recv,
            device_id={"dp": lax.rem(z + k, nz)}, device_id_type=MESH,
        ).start()
        return carry

    lax.fori_loop(1, nz, int_copy, 0)

    def ring_step(view, step):
        for way in range(2):
            if step >= hops[view][way]:
                continue
            ring_copy(view, way, step).wait_recv()
            if step + 1 < hops[view][way]:
                ring_copy(view, way, step + 1).start()
            block = lax.rem(z - 1 - step + nz, nz) if way == 0 else lax.rem(z + 1 + step, nz)
            sib_copy(view, block).start()

    eye = lax.broadcasted_iota(jnp.int32, (LANES, LANES), 0) == lax.broadcasted_iota(jnp.int32, (LANES, LANES), 1)

    def prepare(q):
        c_copies[q].wait()

        def step(i, carry):
            at = pl.ds(pl.multiple_of(i * CH, CH), CH)
            exact, inv = unit_rows(c_raw[at, :])
            c_unit[at, :] = (exact * 1.0).astype(BF16)
            c_inv[at, :] = jnp.broadcast_to(inv, (CH, LANES))
            return carry

        lax.fori_loop(q * quarter // CH, (q + 1) * quarter // CH, step, 0)

    def transpose_units(q):
        def step(i, carry):
            at = pl.ds(pl.multiple_of(i * CH, CH), CH)
            c_unit_t[:, at] = c_unit[at, :].T
            return carry

        lax.fori_loop(q * quarter // CH, (q + 1) * quarter // CH, step, 0)

    def marginal_columns():
        own_copies[4].wait()

        def step(j, carry):
            row = jnp.broadcast_to(marg[pl.ds(j, 1), :], (LANES, LANES))
            column = jnp.sum(jnp.where(eye, row, 0.0), axis=1, keepdims=True)
            marg_col[pl.ds(pl.multiple_of(j * LANES, LANES), LANES), :] = jnp.broadcast_to(column, (LANES, LANES))
            return carry

        lax.fori_loop(0, classes // LANES, step, 0)

    steps = nz // 2
    for s in range(max(steps, 4)):
        if s < 4:
            prepare(s)
        if s < steps:
            for view in range(2):
                ring_step(view, s)
        if s == 0:
            marginal_columns()

    pltpu.make_async_copy(ints_all.at[pl.ds(0, nz - 1)], ints_all.at[pl.ds(0, nz - 1)], int_recv).wait()
    pltpu.make_async_copy(ints_all.at[pl.ds(0, nz - 1)], ints_all.at[pl.ds(0, nz - 1)], int_send).wait()
    offset = (z * ncls + cls) * classes
    for j in range(blocks):
        pair = ints_all[2 * j] + ints_all[2 * j + 1]
        label_row[0:1, j * LANES : (j + 1) * LANES] = pair[0:1, :] - offset
        flag_row[0:1, j * LANES : (j + 1) * LANES] = pair[1:2, :].astype(F32)

    def sib_wait(view):
        whole = views[view].at[pl.ds(0, (nz - 1) * half)]
        pltpu.make_async_copy(whole, whole, sib_recv.at[view]).wait()

    def a_start(n):
        def go(k, carry):
            pltpu.make_async_remote_copy(
                msg_a.at[n], got_a.at[n, cls], a_send.at[n], a_recv.at[n],
                device_id={"cls": lax.rem(cls + k, ncls)}, device_id_type=MESH,
            ).start()
            return carry

        got_a[n, cls] = msg_a[n]
        lax.fori_loop(1, ncls, go, 0)

    def b_start(n):
        whole = got_a.at[n, pl.ds(0, ncls - 1)]
        pltpu.make_async_copy(whole, whole, a_recv.at[n]).wait()
        total = jnp.sum(got_a[n], axis=0)
        msg_b[n] = total
        got_b[n, z] = total

        def go(k, carry):
            pltpu.make_async_remote_copy(
                msg_b.at[n], got_b.at[n, z], b_send.at[n], b_recv.at[n],
                device_id={"dp": lax.rem(z + k, nz)}, device_id_type=MESH,
            ).start()
            return carry

        lax.fori_loop(1, nz, go, 0)

    def b_finish(n):
        whole = got_b.at[n, pl.ds(0, nz - 1)]
        pltpu.make_async_copy(whole, whole, b_recv.at[n]).wait()
        return jnp.sum(got_b[n], axis=0)

    def to_blocks(row, ref, n):
        for j in range(blocks):
            ref[n, j : j + 1, :] = row[:, j * LANES : (j + 1) * LANES]

    def to_row(block, ref):
        for j in range(blocks):
            ref[0:1, j * LANES : (j + 1) * LANES] = block[j : j + 1, :]

    def fold(value):
        return jnp.sum(value.reshape(value.shape[0] // 8, 8, value.shape[1]), axis=0)

    def span(i):
        return pl.ds(pl.multiple_of(i * CH, CH), CH)

    def hits(i):
        ids = lax.broadcasted_iota(jnp.int32, (CH, rows), 0) + i * CH
        return ids == label_row[...]

    n_chunks = classes // CH
    zero = jnp.zeros((8, rows), F32)

    sib_wait(0)

    def teacher_step(i, total):
        at = span(i)
        value = jnp.exp2(nt(c_unit[at, :], weak_all[...]) * LOG2 - LOG2)
        teach[at, :] = value
        return total + fold(value)

    total = lax.fori_loop(0, n_chunks, teacher_step, zero, unroll=2)
    to_blocks(jnp.sum(total, axis=0, keepdims=True), msg_a, 0)
    a_start(0)

    sib_wait(1)

    def student_step(i, carry):
        total, label_dot = carry
        at = span(i)
        hit = hits(i)
        dot = nt(c_unit[at, :], strong_all[...])
        dot = jnp.where(hit, dot - MARGIN, dot)
        stud_dot[at, :] = dot
        value = jnp.exp2(dot * LOG2 - LOG2)
        stud_exp[at, :] = value
        return total + fold(value), label_dot + fold(jnp.where(hit, dot, 0.0))

    carry = lax.fori_loop(0, n_chunks // 2, student_step, (zero, zero), unroll=2)
    b_start(0)
    total, label_dot = lax.fori_loop(n_chunks // 2, n_chunks, student_step, carry, unroll=2)
    to_blocks(jnp.sum(total, axis=0, keepdims=True), msg_a, 1)
    a_start(1)
    to_blocks(SCALE * jnp.sum(label_dot, axis=0, keepdims=True), part_l, 0)
    to_row(1.0 / b_finish(0), vec_t)

    per_row = float(classes * nz * ncls) / rows

    def aligned_step(i, carry):
        q_total, r_total = carry
        at = span(i)
        share = teach[at, :] * vec_t[...]
        batch = per_row * jnp.sum(share, axis=1, keepdims=True)
        fresh = MOMENTUM * marg_col[at, :] + (1.0 - MOMENTUM) * batch
        for j in range(CH // LANES):
            part = fresh[j * LANES : (j + 1) * LANES, :]
            fresh_out[pl.ds(i * (CH // LANES) + j, 1), :] = jnp.sum(jnp.where(eye, part, 0.0), axis=0, keepdims=True)
        inverse = 1.0 / fresh
        raw = share * jnp.concatenate([inverse] * blocks, axis=1)
        teach[at, :] = raw
        return q_total + fold(raw), r_total + fold(raw * stud_dot[at, :])

    carry = lax.fori_loop(0, n_chunks // 2, aligned_step, (zero, zero))
    b_start(1)
    q_total, r_total = lax.fori_loop(n_chunks // 2, n_chunks, aligned_step, carry)
    to_blocks(jnp.sum(q_total, axis=0, keepdims=True), msg_a, 2)
    a_start(2)
    to_blocks(SCALE * jnp.sum(r_total, axis=0, keepdims=True), part_r, 0)
    transpose_units(0)
    transpose_units(1)
    student_total = b_finish(1)
    b_start(2)
    transpose_units(2)
    transpose_units(3)
    aligned_total = b_finish(2)

    to_row(1.0 / student_total, vec_e)
    to_row(-0.5 / aligned_total, vec_q)
    vec_e[...] = vec_e[...] * flag_row[...]
    vec_q[...] = vec_q[...] * flag_row[...]

    def grad_step(i, carry):
        at = span(i)
        value = stud_exp[at, :] * vec_e[...] + teach[at, :] * vec_q[...]
        value = jnp.where(hits(i), value - 0.5 * flag_row[...], value)
        grad_t[at, :] = value.astype(BF16)
        return carry

    lax.fori_loop(0, n_chunks, grad_step, 0, unroll=2)

    flags_block = jnp.concatenate(
        [flag_row[0:1, j * LANES : (j + 1) * LANES] for j in range(blocks)], axis=0
    )
    loss_part = flags_block * (-0.5 * part_l[0] - 0.5 * part_r[0] / aligned_total)
    loss_tile = jnp.concatenate([loss_part, jnp.zeros((8 - blocks, LANES), F32)], axis=0)
    tile_rows = img // 8
    tile_cols = width // 2 // LANES
    per = tile_rows * tile_cols // nplane

    def unit_half(which):
        at = pl.ds(pl.multiple_of(which * (width // 2), width // 2), width // 2)
        out = jnp.dot(c_unit_t[at, :], grad_t[...], preferred_element_type=F32).T
        for block in range(nz):
            for t in range(tile_rows):
                for c in range(tile_cols):
                    index = t * tile_cols + c
                    row = block * img + t * 8
                    half_buf[which, index // per, block * per + index % per] = out[
                        row : row + 8, c * LANES : (c + 1) * LANES
                    ]
        for p in range(nplane):
            half_buf[which, p, nz * per] = loss_tile

    unit_half(1 - core)
    half_copy = pltpu.make_async_remote_copy(
        half_buf.at[1 - core], half_got, half_send, half_recv, device_id={"cls": sibling}, device_id_type=MESH
    )
    half_copy.start()
    unit_half(core)
    half_copy.wait()

    def half_add(p, carry):
        half_buf[core, p] = half_buf[core, p] + half_got[p]
        return carry

    lax.fori_loop(0, nplane, half_add, 0)

    def plane_copy(k, carry):
        p = lax.rem(plane + k, nplane)
        pltpu.make_async_remote_copy(
            half_buf.at[core, p], plane_got.at[plane], plane_send, plane_recv,
            device_id={"cls": p * 2 + core}, device_id_type=MESH,
        ).start()
        return carry

    lax.fori_loop(1, nplane, plane_copy, 0)
    plane_got[plane] = half_buf[core, plane]

    def center_step(i, carry):
        at = span(i)
        value = jnp.dot(grad_t[at, :], strong_all[...], preferred_element_type=F32)
        inverse = jnp.concatenate([c_inv[at, :]] * (width // LANES), axis=1)
        exact = c_raw[at, :].astype(F32) * inverse
        along = jnp.sum(exact * value, axis=1, keepdims=True)
        cgrad_out[at, :] = ((value - exact * along) * inverse).astype(BF16)
        return carry

    third = n_chunks * 5 // 8
    lax.fori_loop(0, third, center_step, 0, unroll=2)

    whole = plane_got.at[pl.ds(0, nplane - 1)]
    pltpu.make_async_copy(whole, whole, plane_recv).wait()
    plane_sum = jnp.sum(plane_got[...], axis=0)
    for block in range(nz):
        z_send[block, 0:per] = plane_sum[block * per : (block + 1) * per]
        z_send[block, per] = plane_sum[nz * per]
    z_got[z] = z_send[z]

    def z_copy(k, carry):
        to = lax.rem(z + k, nz)
        pltpu.make_async_remote_copy(
            z_send.at[to], z_got.at[z], z_send_sem, z_recv_sem, device_id={"dp": to}, device_id_type=MESH
        ).start()
        return carry

    lax.fori_loop(1, nz, z_copy, 0)

    two = n_chunks * 7 // 8
    lax.fori_loop(third, two, center_step, 0, unroll=2)

    whole_z = z_got.at[pl.ds(0, nz - 1)]
    pltpu.make_async_copy(whole_z, whole_z, z_recv_sem).wait()
    z_sum = jnp.sum(z_got[...], axis=0)
    tile_own[...] = z_sum[0:per]
    tile_got[cls] = z_sum[0:per]

    def tile_copy(k, carry):
        pltpu.make_async_remote_copy(
            tile_own, tile_got.at[cls], tile_send, tile_recv,
            device_id={"cls": lax.rem(cls + k, ncls)}, device_id_type=MESH,
        ).start()
        return carry

    lax.fori_loop(1, ncls, tile_copy, 0)

    lax.fori_loop(two, n_chunks, center_step, 0, unroll=2)

    loss_rows = flags_block * (SCALE + jnp.log(student_total)) + z_sum[per, 0:blocks, :]
    loss_out[...] = jnp.sum(jnp.sum(loss_rows, axis=1, keepdims=True), axis=0, keepdims=True) / img

    whole_t = tile_got.at[pl.ds(0, ncls - 1)]
    pltpu.make_async_copy(whole_t, whole_t, tile_recv).wait()
    bands = []
    for t in range(tile_rows):
        tiles = []
        for c in range(2 * tile_cols):
            index = t * tile_cols + c % tile_cols
            tiles.append(tile_got[(index // per) * 2 + c // tile_cols, index % per])
        bands.append(jnp.concatenate(tiles, axis=1))
    unit_grad = jnp.concatenate(bands, axis=0)
    exact, inverse = unit_rows(strong_own[...])
    egrad_out[...] = (unit_grad - exact * jnp.sum(exact * unit_grad, axis=1, keepdims=True)) * inverse

    for view in range(2):
        for way in range(2):
            for step in range(hops[view][way]):
                ring_copy(view, way, step).wait_send()
        sent = views[view].at[pl.ds(0, (nz - 1) * half)]
        pltpu.make_async_copy(sent, sent, sib_send.at[view]).wait()
    for n in range(3):
        sent = got_a.at[n, pl.ds(0, ncls - 1)]
        pltpu.make_async_copy(sent, sent, a_send.at[n]).wait()
        sent = got_b.at[n, pl.ds(0, nz - 1)]
        pltpu.make_async_copy(sent, sent, b_send.at[n]).wait()
    pltpu.make_async_copy(whole, whole, plane_send).wait()
    pltpu.make_async_copy(whole_z, whole_z, z_send_sem).wait()
    pltpu.make_async_copy(whole_t, whole_t, tile_send).wait()


def body(nz, ncls, weak_embed, strong_embed, centers, marginal, pseudo_label, confident):
    img, width = weak_embed.shape
    classes = centers.shape[0]
    rows = img * nz
    blocks = rows // LANES
    nplane = ncls // 2
    per = (img // 8) * (width // 2 // LANES) // nplane
    vmem = pltpu.VMEM
    dma = pltpu.SemaphoreType.DMA
    hop = nz // 2
    scratch = [
        vmem((img, width), BF16), vmem((img, width), BF16), vmem((2, img), jnp.int32), vmem((classes // LANES, LANES), F32),
        vmem((rows, width), BF16), vmem((rows, width), BF16), vmem((nz, 2, LANES), jnp.int32),
        vmem((1, rows), jnp.int32), vmem((1, rows), F32),
        vmem((classes, width), BF16), vmem((classes, width), BF16), vmem((width, classes), BF16),
        vmem((classes, LANES), F32), vmem((classes, LANES), F32),
        vmem((classes, rows), F32), vmem((classes, rows), F32), vmem((classes, rows), F32), vmem((classes, rows), BF16),
        vmem((1, rows), F32), vmem((1, rows), F32), vmem((1, rows), F32),
        vmem((3, blocks, LANES), F32), vmem((3, blocks, LANES), F32),
        vmem((3, ncls, blocks, LANES), F32), vmem((3, nz, blocks, LANES), F32),
        vmem((1, blocks, LANES), F32), vmem((1, blocks, LANES), F32),
        vmem((2, nplane, nz * per + 1, 8, LANES), F32), vmem((nplane, nz * per + 1, 8, LANES), F32),
        vmem((nplane, nz * per + 1, 8, LANES), F32),
        vmem((nz, per + 1, 8, LANES), F32), vmem((nz, per + 1, 8, LANES), F32),
        vmem((per, 8, LANES), F32), vmem((ncls, per, 8, LANES), F32),
        dma((5,)), dma((4,)),
        dma((2, 2, hop)), dma((2, 2, hop)), dma((2,)), dma((2,)), dma, dma,
        dma((3,)), dma((3,)), dma((3,)), dma((3,)),
        dma, dma, dma, dma, dma, dma, dma, dma,
    ]
    hbm = pl.BlockSpec(memory_space=pl.ANY)
    local = pl.BlockSpec(memory_space=pltpu.VMEM)
    fresh, cgrad, egrad, loss = pl.pallas_call(
        functools.partial(kernel, nz, ncls),
        out_shape=(
            jax.ShapeDtypeStruct((classes // LANES, LANES), F32),
            jax.ShapeDtypeStruct((classes, width), BF16),
            jax.ShapeDtypeStruct((img, width), F32),
            jax.ShapeDtypeStruct((1, 1), F32),
        ),
        in_specs=[hbm] * 6,
        out_specs=(local,) * 4,
        scratch_shapes=scratch,
        compiler_params=pltpu.CompilerParams(
            collective_id=0, has_side_effects=True, vmem_limit_bytes=55 * 1024 * 1024
        ),
    )(
        weak_embed, strong_embed, centers, marginal.reshape(classes // LANES, LANES),
        pseudo_label.reshape(1, img), confident.reshape(1, img),
    )
    return fresh.reshape(classes), cgrad, egrad, loss.reshape(())


def solution(mesh):
    placed = (
        P("dp", None),
        P("dp", None),
        P(("dp", "cls"), None),
        P(("dp", "cls")),
        P("dp"),
        P("dp"),
    )
    return jax.shard_map(
        functools.partial(body, mesh.shape["dp"], mesh.shape["cls"]),
        mesh=mesh,
        in_specs=placed,
        out_specs=(P(("dp", "cls")), P(("dp", "cls"), None), P("dp", None), P()),
        check_vma=False,
    )
```

time: 509 us -> 89.4 us (0.18)
  waiting for transfers between devices: 246 us -> 0 us
  blocking collectives: 168 us -> 0 us
  Pallas kernels: 0 us -> 80.2 us
  other arithmetic: 39.3 us -> 0 us
  matrix products: 16.4 us -> 0 us
  local copies, waits for them, and re-layouts: 21.5 us -> 6.49 us
  between operations: 16.7 us -> 2.45 us
    psum x1 -> x0, waiting for transfers between devices: 234 us -> none  [body(): unit_total = lax.psum(unit_part, ('dp', 'cls'))]
    psum x2 -> x0, blocking collectives: 153 us -> none  [the longest x1 79.6 us: body(): teacher_total = lax.psum(teach_part, ('dp', 'cls'))]
    pallas_call x0 -> x1, Pallas kernels: none -> 80.2 us  [body(): pl.pallas_call(functools.partial(kernel, nz, ncls), out_shape=(jax.ShapeD...]
    reduce_sum x8 -> x0, other arithmetic: 22.8 us -> none  [the longest x1 10.2 us: body(): label_part = jnp.sum(hit * stud, axis=1)]
    dot_general x3 -> x0, matrix products: 16.4 us -> none  [the longest x1 6.59 us: body(): lax.dot_general(views.reshape(2 * row_count, width), center_unit, (((1,),...]
    unnamed x29 -> x5, local copies, waits for them, and re-layouts: 21.5 us -> 6.49 us
    unnamed x1 -> x0, blocking collectives: 14.1 us -> none
    convert_element_type x3 -> x0, other arithmetic: 13.2 us -> none  [the longest x1 9.62 us: body(): grad = grad.astype(jnp.bfloat16)]
  transfers between devices with their start and end apart: 2 -> 0, of which waited for: 2 -> 0; matrix products, arithmetic and copies ran while one was open for 5% -> 0% of each run, Pallas kernels for 0% -> 0%
where the time goes in v1:
time: 89.4 us; the launch traced here: 89.2 us
  Pallas kernels  80.2 us (90%)
  local copies, waits for them, and re-layouts  6.49 us (7%)
  between operations  2.45 us (3%)
    pallas_call x1, Pallas kernels, body(): pl.pallas_call(functools.partial(kernel, nz, ncls), out_shape=(jax.ShapeD...  80.2 us
    unnamed x5, local copies, waits for them, and re-layouts  6.49 us

profile of v1, /device:TPU:1, one launch (start us, length us, event | category | flops | bytes accessed | tf_op | source)
XLA Modules:
  0.0 89.2 jit_solution(17517685283543917166)
XLA Ops:
  0.6 80.2 %shard_map.93 = (f32[32,128]{1,0:T(8,128)}, bf16[4096,512]{1,0:T(8,128)(2,1)}, f32[64,512]{1,0:T(8,128)}, f32[1,1]{1,0:T(1,128)}) custom-call(bf16[64,512]{1,0:T(8,128)(2,1)} %weak_hbm.1, bf16[64,512]{1,0:T(8,128)(2,1)} %strong_hbm.1, bf16[4096,512]{1,0:T(8,128)(2,1)} %centers_hbm.1, f32[32,128]{1,0:T(8,128)} %bitcast.5, s32[1,64]{1,0:T(1,128)} %bitcast.7, ...), custom_call_target="tpu_custom_call" | custom-call | tf_op jit(solution)/shard_map/pallas_call | solution.py:500
  80.9 1.3 %copy.14 = f32[4096]{0:T(1024)} copy(f32[4096]{0:T(1024)} %bitcast.6) | data formatting | bytes 32768
  82.2 0.0 copy-start
  82.2 4.5 %copy.15 = bf16[4096,512]{1,0:T(8,128)(2,1)} copy(bf16[4096,512]{1,0:T(8,128)(2,1)} %get-tuple-element.17) | data formatting | bytes 8388608
  86.7 0.0 copy-done
  86.7 0.7 copy.16
Async XLA Ops:
  82.2 4.5 %copy-start = (f32[64,512]{1,0:T(8,128)S(1)}, f32[64,512]{1,0:T(8,128)}, u32[]{:S(2)}) copy-start(f32[64,512]{1,0:T(8,128)} %get-tuple-element.18) | copy-start | bytes 393220

commit v2 on v1

--- a/solution.py
+++ b/solution.py
@@ -17,6 +17,8 @@
 F32 = jnp.float32
 BF16 = jnp.bfloat16
 CH = 256
+TCH, TUN = 256, 4
+SCH, SUN = 256, 4
 LANES = 128
 
 
@@ -42,7 +44,7 @@
     msg_a, msg_b, got_a, got_b,
     part_l, part_r, half_buf, half_got, plane_got, z_send, z_got, tile_own, tile_got,
     in_sem, c_sem,
-    ring_send, ring_recv, sib_send, sib_recv, int_send, int_recv,
+    gather_send, gather_recv, sib_send, sib_recv, int_send, int_recv,
     a_send, a_recv, b_send, b_recv,
     half_send, half_recv, plane_send, plane_recv, z_send_sem, z_recv_sem, tile_send, tile_recv,
 ):
@@ -90,66 +92,70 @@
 
     lax.fori_loop(1, nz, greet_z, 0)
     lax.fori_loop(1, ncls, greet_cls, 0)
-
+    base = pl.multiple_of(z * img, img)
     own_copies[0].wait()
-    own_copies[1].wait()
-    base = pl.multiple_of(z * img, img)
     weak_exact, _ = unit_rows(weak_own[...])
     weak_all[pl.ds(base, img), :] = weak_exact.astype(BF16)
-    strong_exact, strong_inv = unit_rows(strong_own[...])
+    pl.semaphore_wait(barrier, nz - 1 + ncls - 1)
+
+    views = (weak_all, strong_all)
+    near = nz // 2
+    group, seat = lax.div(z, near), lax.rem(z, near)
+    sends = [(away, k) for away in range(2) for k in range(near) if away or k]
+
+    def piece(view, block):
+        return views[view].at[pl.ds(pl.multiple_of(block * img + core * half, half), half)]
+
+    def gather_copy(view, away, k):
+        ref = piece(view, z)
+        to = lax.rem(group + away, 2) * near + lax.rem(seat + k, near)
+        at = away * near + k
+        return pltpu.make_async_remote_copy(
+            ref, ref, gather_send.at[view, at], gather_recv.at[view, at],
+            device_id={"dp": to}, device_id_type=MESH,
+        )
+
+    def sib_copy(view, away, k):
+        ref = piece(view, lax.rem(group + away, 2) * near + lax.rem(seat + near - k, near))
+        return pltpu.make_async_remote_copy(
+            ref, ref, sib_send.at[view, away], sib_recv.at[view, away],
+            device_id={"cls": sibling}, device_id_type=MESH,
+        )
+
+    def int_copy(k, carry):
+        pltpu.make_async_remote_copy(
+            ints_all.at[z], ints_all.at[z], int_send, int_recv,
+            device_id={"dp": lax.rem(z + k, nz)}, device_id_type=MESH,
+        ).start()
+        return carry
+
+    for away, k in sends:
+        gather_copy(0, away, k).start()
+    own_copies[1].wait()
+    strong_exact, _ = unit_rows(strong_own[...])
     strong_all[pl.ds(base, img), :] = strong_exact.astype(BF16)
+    for away, k in sends:
+        gather_copy(1, away, k).start()
     own_copies[2].wait()
     own_copies[3].wait()
     mine = ints_own[:, 0:img]
     both = jnp.concatenate([mine, mine], axis=1)
     lane = lax.broadcasted_iota(jnp.int32, both.shape, 1)
     ints_all[z] = jnp.where(lax.div(lane, img) == lax.rem(z, 2), both, 0)
-
-    pl.semaphore_wait(barrier, nz - 1 + ncls - 1)
-
-    views = (weak_all, strong_all)
-    hops = [(nz // 2, nz - 1 - nz // 2), (nz - 1 - nz // 2, nz // 2)]
-
-    def piece(view, block):
-        return views[view].at[pl.ds(pl.multiple_of(block * img + core * half, half), half)]
-
-    def ring_copy(view, way, step):
-        block = lax.rem(z - step + nz, nz) if way == 0 else lax.rem(z + step, nz)
-        to = lax.rem(z + 1, nz) if way == 0 else lax.rem(z + nz - 1, nz)
-        ref = piece(view, block)
-        return pltpu.make_async_remote_copy(
-            ref, ref, ring_send.at[view, way, step], ring_recv.at[view, way, step],
-            device_id={"dp": to}, device_id_type=MESH,
-        )
-
-    def sib_copy(view, block):
-        ref = piece(view, block)
-        return pltpu.make_async_remote_copy(
-            ref, ref, sib_send.at[view], sib_recv.at[view], device_id={"cls": sibling}, device_id_type=MESH
-        )
-
-    for view in range(2):
-        for way in range(2):
-            ring_copy(view, way, 0).start()
-
-    def int_copy(k, carry):
-        pltpu.make_async_remote_copy(
-            ints_all.at[z], ints_all.at[z], int_send, int_recv,
-            device_id={"dp": lax.rem(z + k, nz)}, device_id_type=MESH,
-        ).start()
-        return carry
-
     lax.fori_loop(1, nz, int_copy, 0)
 
-    def ring_step(view, step):
-        for way in range(2):
-            if step >= hops[view][way]:
-                continue
-            ring_copy(view, way, step).wait_recv()
-            if step + 1 < hops[view][way]:
-                ring_copy(view, way, step + 1).start()
-            block = lax.rem(z - 1 - step + nz, nz) if way == 0 else lax.rem(z + 1 + step, nz)
-            sib_copy(view, block).start()
+    def pass_on(view, away):
+        for k in range(near):
+            if away or k:
+                gather_copy(view, away, k).wait_recv()
+                sib_copy(view, away, k).start()
+
+    def sib_whole(view, away):
+        return views[view].at[pl.ds(0, (near if away else near - 1) * half)]
+
+    def sib_wait(view, away):
+        whole = sib_whole(view, away)
+        pltpu.make_async_copy(whole, whole, sib_recv.at[view, away]).wait()
 
     eye = lax.broadcasted_iota(jnp.int32, (LANES, LANES), 0) == lax.broadcasted_iota(jnp.int32, (LANES, LANES), 1)
 
@@ -184,27 +190,9 @@
 
         lax.fori_loop(0, classes // LANES, step, 0)
 
-    steps = nz // 2
-    for s in range(max(steps, 4)):
-        if s < 4:
-            prepare(s)
-        if s < steps:
-            for view in range(2):
-                ring_step(view, s)
-        if s == 0:
-            marginal_columns()
-
-    pltpu.make_async_copy(ints_all.at[pl.ds(0, nz - 1)], ints_all.at[pl.ds(0, nz - 1)], int_recv).wait()
-    pltpu.make_async_copy(ints_all.at[pl.ds(0, nz - 1)], ints_all.at[pl.ds(0, nz - 1)], int_send).wait()
-    offset = (z * ncls + cls) * classes
-    for j in range(blocks):
-        pair = ints_all[2 * j] + ints_all[2 * j + 1]
-        label_row[0:1, j * LANES : (j + 1) * LANES] = pair[0:1, :] - offset
-        flag_row[0:1, j * LANES : (j + 1) * LANES] = pair[1:2, :].astype(F32)
-
-    def sib_wait(view):
-        whole = views[view].at[pl.ds(0, (nz - 1) * half)]
-        pltpu.make_async_copy(whole, whole, sib_recv.at[view]).wait()
+    for q in range(4):
+        prepare(q)
+    marginal_columns()
 
     def a_start(n):
         def go(k, carry):
@@ -249,44 +237,62 @@
     def fold(value):
         return jnp.sum(value.reshape(value.shape[0] // 8, 8, value.shape[1]), axis=0)
 
-    def span(i):
-        return pl.ds(pl.multiple_of(i * CH, CH), CH)
-
-    def hits(i):
-        ids = lax.broadcasted_iota(jnp.int32, (CH, rows), 0) + i * CH
+    def span(i, size=CH):
+        return pl.ds(pl.multiple_of(i * size, size), size)
+
+    def hits(i, size=CH):
+        ids = lax.broadcasted_iota(jnp.int32, (size, rows), 0) + i * size
         return ids == label_row[...]
 
     n_chunks = classes // CH
     zero = jnp.zeros((8, rows), F32)
 
-    sib_wait(0)
-
-    def teacher_step(i, total):
-        at = span(i)
-        value = jnp.exp2(nt(c_unit[at, :], weak_all[...]) * LOG2 - LOG2)
-        teach[at, :] = value
-        return total + fold(value)
-
-    total = lax.fori_loop(0, n_chunks, teacher_step, zero, unroll=2)
-    to_blocks(jnp.sum(total, axis=0, keepdims=True), msg_a, 0)
+    group_rows = rows // 2
+
+    for away in range(2):
+        pass_on(0, away)
+        sib_wait(0, away)
+        lanes = pl.ds(pl.multiple_of(lax.rem(group + away, 2) * group_rows, group_rows), group_rows)
+
+        def teacher_step(i, total):
+            at = span(i, TCH)
+            value = jnp.exp2(nt(c_unit[at, :], weak_all[lanes, :]) * LOG2 - LOG2)
+            teach[at, lanes] = value
+            return total + fold(value)
+
+        total = lax.fori_loop(0, classes // TCH, teacher_step, jnp.zeros((8, group_rows), F32), unroll=TUN)
+        vec_t[0:1, lanes] = jnp.sum(total, axis=0, keepdims=True)
+    to_blocks(vec_t[...], msg_a, 0)
     a_start(0)
 
-    sib_wait(1)
+    others = ints_all.at[pl.ds(0, nz - 1)]
+    pltpu.make_async_copy(others, others, int_recv).wait()
+    pltpu.make_async_copy(others, others, int_send).wait()
+    offset = (z * ncls + cls) * classes
+    for j in range(blocks):
+        pair = ints_all[2 * j] + ints_all[2 * j + 1]
+        label_row[0:1, j * LANES : (j + 1) * LANES] = pair[0:1, :] - offset
+        flag_row[0:1, j * LANES : (j + 1) * LANES] = pair[1:2, :].astype(F32)
+
+    for q in range(4):
+        transpose_units(q)
+    for away in range(2):
+        pass_on(1, away)
+    b_start(0)
+    for away in range(2):
+        sib_wait(1, away)
 
     def student_step(i, carry):
         total, label_dot = carry
-        at = span(i)
-        hit = hits(i)
+        at = span(i, SCH)
+        hit = hits(i, SCH)
         dot = nt(c_unit[at, :], strong_all[...])
         dot = jnp.where(hit, dot - MARGIN, dot)
         stud_dot[at, :] = dot
         value = jnp.exp2(dot * LOG2 - LOG2)
         stud_exp[at, :] = value
         return total + fold(value), label_dot + fold(jnp.where(hit, dot, 0.0))
-
-    carry = lax.fori_loop(0, n_chunks // 2, student_step, (zero, zero), unroll=2)
-    b_start(0)
-    total, label_dot = lax.fori_loop(n_chunks // 2, n_chunks, student_step, carry, unroll=2)
+    total, label_dot = lax.fori_loop(0, classes // SCH, student_step, (zero, zero), unroll=SUN)
     to_blocks(jnp.sum(total, axis=0, keepdims=True), msg_a, 1)
     a_start(1)
     to_blocks(SCALE * jnp.sum(label_dot, axis=0, keepdims=True), part_l, 0)
@@ -294,8 +300,7 @@
 
     per_row = float(classes * nz * ncls) / rows
 
-    def aligned_step(i, carry):
-        q_total, r_total = carry
+    def aligned_step(i, q_total):
         at = span(i)
         share = teach[at, :] * vec_t[...]
         batch = per_row * jnp.sum(share, axis=1, keepdims=True)
@@ -306,35 +311,33 @@
         inverse = 1.0 / fresh
         raw = share * jnp.concatenate([inverse] * blocks, axis=1)
         teach[at, :] = raw
-        return q_total + fold(raw), r_total + fold(raw * stud_dot[at, :])
-
-    carry = lax.fori_loop(0, n_chunks // 2, aligned_step, (zero, zero))
-    b_start(1)
-    q_total, r_total = lax.fori_loop(n_chunks // 2, n_chunks, aligned_step, carry)
+        return q_total + fold(raw)
+    q_total = lax.fori_loop(0, n_chunks, aligned_step, zero, unroll=2)
     to_blocks(jnp.sum(q_total, axis=0, keepdims=True), msg_a, 2)
     a_start(2)
+
+    def cross_step(i, r_total):
+        at = span(i)
+        return r_total + fold(teach[at, :] * stud_dot[at, :])
+
+    r_total = lax.fori_loop(0, n_chunks, cross_step, zero, unroll=2)
     to_blocks(SCALE * jnp.sum(r_total, axis=0, keepdims=True), part_r, 0)
-    transpose_units(0)
-    transpose_units(1)
+    b_start(1)
+    b_start(2)
     student_total = b_finish(1)
-    b_start(2)
-    transpose_units(2)
-    transpose_units(3)
+    to_row(1.0 / student_total, vec_e)
+    vec_e[...] = vec_e[...] * flag_row[...]
+
+    def share_step(i, carry):
+        at = span(i)
+        value = stud_exp[at, :] * vec_e[...]
+        stud_exp[at, :] = jnp.where(hits(i), value - 0.5 * flag_row[...], value)
+        return carry
+
+    lax.fori_loop(0, n_chunks, share_step, 0, unroll=2)
     aligned_total = b_finish(2)
-
-    to_row(1.0 / student_total, vec_e)
     to_row(-0.5 / aligned_total, vec_q)
-    vec_e[...] = vec_e[...] * flag_row[...]
     vec_q[...] = vec_q[...] * flag_row[...]
-
-    def grad_step(i, carry):
-        at = span(i)
-        value = stud_exp[at, :] * vec_e[...] + teach[at, :] * vec_q[...]
-        value = jnp.where(hits(i), value - 0.5 * flag_row[...], value)
-        grad_t[at, :] = value.astype(BF16)
-        return carry
-
-    lax.fori_loop(0, n_chunks, grad_step, 0, unroll=2)
 
     flags_block = jnp.concatenate(
         [flag_row[0:1, j * LANES : (j + 1) * LANES] for j in range(blocks)], axis=0
@@ -344,45 +347,65 @@
     tile_rows = img // 8
     tile_cols = width // 2 // LANES
     per = tile_rows * tile_cols // nplane
-
-    def unit_half(which):
+    last = near * per
+
+    def half_copy(part):
+        return pltpu.make_async_remote_copy(
+            half_buf.at[part, 1 - core], half_got.at[part], half_send.at[part], half_recv.at[part],
+            device_id={"cls": sibling}, device_id_type=MESH,
+        )
+
+    def unit_half(part, which):
         at = pl.ds(pl.multiple_of(which * (width // 2), width // 2), width // 2)
-        out = jnp.dot(c_unit_t[at, :], grad_t[...], preferred_element_type=F32).T
-        for block in range(nz):
+        lanes = pl.ds(part * group_rows, group_rows)
+        out = jnp.dot(c_unit_t[at, :], grad_t[:, lanes], preferred_element_type=F32).T
+        for block in range(near):
             for t in range(tile_rows):
                 for c in range(tile_cols):
                     index = t * tile_cols + c
                     row = block * img + t * 8
-                    half_buf[which, index // per, block * per + index % per] = out[
+                    half_buf[part, which, index // per, block * per + index % per] = out[
                         row : row + 8, c * LANES : (c + 1) * LANES
                     ]
         for p in range(nplane):
-            half_buf[which, p, nz * per] = loss_tile
-
-    unit_half(1 - core)
-    half_copy = pltpu.make_async_remote_copy(
-        half_buf.at[1 - core], half_got, half_send, half_recv, device_id={"cls": sibling}, device_id_type=MESH
-    )
-    half_copy.start()
-    unit_half(core)
-    half_copy.wait()
-
-    def half_add(p, carry):
-        half_buf[core, p] = half_buf[core, p] + half_got[p]
-        return carry
-
-    lax.fori_loop(0, nplane, half_add, 0)
-
-    def plane_copy(k, carry):
-        p = lax.rem(plane + k, nplane)
-        pltpu.make_async_remote_copy(
-            half_buf.at[core, p], plane_got.at[plane], plane_send, plane_recv,
-            device_id={"cls": p * 2 + core}, device_id_type=MESH,
-        ).start()
-        return carry
-
-    lax.fori_loop(1, nplane, plane_copy, 0)
-    plane_got[plane] = half_buf[core, plane]
+            half_buf[part, which, p, last] = loss_tile
+
+    def plane_start(part):
+        half_copy(part).wait_recv()
+
+        def half_add(p, carry):
+            half_buf[part, core, p] = half_buf[part, core, p] + half_got[part, p]
+            return carry
+
+        lax.fori_loop(0, nplane, half_add, 0, unroll=True)
+
+        def plane_copy(k, carry):
+            p = lax.rem(plane + k, nplane)
+            pltpu.make_async_remote_copy(
+                half_buf.at[part, core, p], plane_got.at[part, plane], plane_send.at[part], plane_recv.at[part],
+                device_id={"cls": p * 2 + core}, device_id_type=MESH,
+            ).start()
+            return carry
+
+        lax.fori_loop(1, nplane, plane_copy, 0)
+        plane_got[part, plane] = half_buf[part, core, plane]
+
+    for part in range(2):
+        lanes = pl.ds(part * group_rows, group_rows)
+
+        def grad_step(i, carry):
+            at = span(i)
+            value = stud_exp[at, lanes] + teach[at, lanes] * vec_q[0:1, lanes]
+            grad_t[at, lanes] = value.astype(BF16)
+            return carry
+
+        lax.fori_loop(0, n_chunks, grad_step, 0, unroll=2)
+        if part == 1:
+            plane_start(0)
+        unit_half(part, 1 - core)
+        half_copy(part).start()
+        unit_half(part, core)
+    plane_start(1)
 
     def center_step(i, carry):
         at = span(i)
@@ -396,12 +419,14 @@
     third = n_chunks * 5 // 8
     lax.fori_loop(0, third, center_step, 0, unroll=2)
 
-    whole = plane_got.at[pl.ds(0, nplane - 1)]
-    pltpu.make_async_copy(whole, whole, plane_recv).wait()
-    plane_sum = jnp.sum(plane_got[...], axis=0)
+    for part in range(2):
+        whole = plane_got.at[part, pl.ds(0, nplane - 1)]
+        pltpu.make_async_copy(whole, whole, plane_recv.at[part]).wait()
+        plane_sum = jnp.sum(plane_got[part], axis=0)
+        for block in range(near):
+            z_send[part * near + block, 0:per] = plane_sum[block * per : (block + 1) * per]
     for block in range(nz):
-        z_send[block, 0:per] = plane_sum[block * per : (block + 1) * per]
-        z_send[block, per] = plane_sum[nz * per]
+        z_send[block, per] = plane_sum[last]
     z_got[z] = z_send[z]
 
     def z_copy(k, carry):
@@ -430,9 +455,7 @@
         return carry
 
     lax.fori_loop(1, ncls, tile_copy, 0)
-
     lax.fori_loop(two, n_chunks, center_step, 0, unroll=2)
-
     loss_rows = flags_block * (SCALE + jnp.log(student_total)) + z_sum[per, 0:blocks, :]
     loss_out[...] = jnp.sum(jnp.sum(loss_rows, axis=1, keepdims=True), axis=0, keepdims=True) / img
 
@@ -448,21 +471,32 @@
     unit_grad = jnp.concatenate(bands, axis=0)
     exact, inverse = unit_rows(strong_own[...])
     egrad_out[...] = (unit_grad - exact * jnp.sum(exact * unit_grad, axis=1, keepdims=True)) * inverse
-
     for view in range(2):
-        for way in range(2):
-            for step in range(hops[view][way]):
-                ring_copy(view, way, step).wait_send()
-        sent = views[view].at[pl.ds(0, (nz - 1) * half)]
-        pltpu.make_async_copy(sent, sent, sib_send.at[view]).wait()
+        for away, k in sends:
+            gather_copy(view, away, k).wait_send()
+        for away in range(2):
+            sent = sib_whole(view, away)
+            pltpu.make_async_copy(sent, sent, sib_send.at[view, away]).wait()
     for n in range(3):
         sent = got_a.at[n, pl.ds(0, ncls - 1)]
         pltpu.make_async_copy(sent, sent, a_send.at[n]).wait()
         sent = got_b.at[n, pl.ds(0, nz - 1)]
         pltpu.make_async_copy(sent, sent, b_send.at[n]).wait()
-    pltpu.make_async_copy(whole, whole, plane_send).wait()
+    for part in range(2):
+        half_copy(part).wait_send()
+        sent = plane_got.at[part, pl.ds(0, nplane - 1)]
+        pltpu.make_async_copy(sent, sent, plane_send.at[part]).wait()
     pltpu.make_async_copy(whole_z, whole_z, z_send_sem).wait()
     pltpu.make_async_copy(whole_t, whole_t, tile_send).wait()
+
+
+def store(fresh_in, cgrad_in, egrad_in, loss_in, fresh_out, cgrad_out, egrad_out, loss_out, sem):
+    parts = ((cgrad_in, cgrad_out), (egrad_in, egrad_out), (fresh_in, fresh_out), (loss_in, loss_out))
+    copies = [pltpu.make_async_copy(a, b, sem.at[n]) for n, (a, b) in enumerate(parts)]
+    for copy in copies:
+        copy.start()
+    for copy in copies:
+        copy.wait()
 
 
 def body(nz, ncls, weak_embed, strong_embed, centers, marginal, pseudo_label, confident):
@@ -474,7 +508,6 @@
     per = (img // 8) * (width // 2 // LANES) // nplane
     vmem = pltpu.VMEM
     dma = pltpu.SemaphoreType.DMA
-    hop = nz // 2
     scratch = [
         vmem((img, width), BF16), vmem((img, width), BF16), vmem((2, img), jnp.int32), vmem((classes // LANES, LANES), F32),
         vmem((rows, width), BF16), vmem((rows, width), BF16), vmem((nz, 2, LANES), jnp.int32),
@@ -486,25 +519,21 @@
         vmem((3, blocks, LANES), F32), vmem((3, blocks, LANES), F32),
         vmem((3, ncls, blocks, LANES), F32), vmem((3, nz, blocks, LANES), F32),
         vmem((1, blocks, LANES), F32), vmem((1, blocks, LANES), F32),
-        vmem((2, nplane, nz * per + 1, 8, LANES), F32), vmem((nplane, nz * per + 1, 8, LANES), F32),
-        vmem((nplane, nz * per + 1, 8, LANES), F32),
+        vmem((2, 2, nplane, nz // 2 * per + 1, 8, LANES), F32), vmem((2, nplane, nz // 2 * per + 1, 8, LANES), F32),
+        vmem((2, nplane, nz // 2 * per + 1, 8, LANES), F32),
         vmem((nz, per + 1, 8, LANES), F32), vmem((nz, per + 1, 8, LANES), F32),
         vmem((per, 8, LANES), F32), vmem((ncls, per, 8, LANES), F32),
         dma((5,)), dma((4,)),
-        dma((2, 2, hop)), dma((2, 2, hop)), dma((2,)), dma((2,)), dma, dma,
+        dma((2, nz)), dma((2, nz)), dma((2, 2)), dma((2, 2)), dma, dma,
         dma((3,)), dma((3,)), dma((3,)), dma((3,)),
-        dma, dma, dma, dma, dma, dma, dma, dma,
+        dma((2,)), dma((2,)), dma((2,)), dma((2,)), dma, dma, dma, dma,
     ]
     hbm = pl.BlockSpec(memory_space=pl.ANY)
     local = pl.BlockSpec(memory_space=pltpu.VMEM)
-    fresh, cgrad, egrad, loss = pl.pallas_call(
+    shapes = (((classes // LANES, LANES), F32), ((classes, width), BF16), ((img, width), F32), ((1, 1), F32))
+    results = pl.pallas_call(
         functools.partial(kernel, nz, ncls),
-        out_shape=(
-            jax.ShapeDtypeStruct((classes // LANES, LANES), F32),
-            jax.ShapeDtypeStruct((classes, width), BF16),
-            jax.ShapeDtypeStruct((img, width), F32),
-            jax.ShapeDtypeStruct((1, 1), F32),
-        ),
+        out_shape=tuple(pltpu.VMEM(*shape) for shape in shapes),
         in_specs=[hbm] * 6,
         out_specs=(local,) * 4,
         scratch_shapes=scratch,
@@ -515,6 +544,14 @@
         weak_embed, strong_embed, centers, marginal.reshape(classes // LANES, LANES),
         pseudo_label.reshape(1, img), confident.reshape(1, img),
     )
+    fresh, cgrad, egrad, loss = pl.pallas_call(
+        store,
+        out_shape=tuple(jax.ShapeDtypeStruct(*shape) for shape in shapes),
+        in_specs=[local] * 4,
+        out_specs=(hbm,) * 4,
+        scratch_shapes=[dma((4,))],
+        compiler_params=pltpu.CompilerParams(vmem_limit_bytes=1024 * 1024),
+    )(*results)
     return fresh.reshape(classes), cgrad, egrad, loss.reshape(())
 
 

time: 89.4 us -> 74.8 us (0.84)
  local copies, waits for them, and re-layouts: 6.49 us -> 0 us
  Pallas kernels: 80.2 us -> 74.1 us
  between operations: 2.45 us -> 0.64 us
    unnamed x5 -> x0, local copies, waits for them, and re-layouts: 6.49 us -> none
    pallas_call x1 -> x2, Pallas kernels: 80.2 us -> 74.1 us  [the longest x1 71.4 us: body(): pl.pallas_call(functools.partial(kernel, nz, ncls), out_shape=tuple((pltp...]
where the time goes in v2:
time: 74.8 us; the launch traced here: 74.7 us
  Pallas kernels  74.1 us (99%)
    pallas_call x1, Pallas kernels, body(): pl.pallas_call(functools.partial(kernel, nz, ncls), out_shape=tuple((pltp...  71.4 us
    pallas_call x1, Pallas kernels, body(): pl.pallas_call(store, out_shape=tuple((jax.ShapeDtypeStruct(*shape) for s...  2.71 us

profile of v2, /device:TPU:1, one launch (start us, length us, event | category | flops | bytes accessed | tf_op | source)
XLA Modules:
  0.0 74.7 jit_solution(6233969453836847887)
XLA Ops:
  0.6 71.4 %shard_map.93 = (f32[32,128]{1,0:T(8,128)S(1)}, bf16[4096,512]{1,0:T(8,128)(2,1)S(1)}, f32[64,512]{1,0:T(8,128)S(1)}, f32[1,1]{1,0:T(1,128)}) custom-call(bf16[64,512]{1,0:T(8,128)(2,1)} %weak_hbm.1, bf16[64,512]{1,0:T(8,128)(2,1)} %strong_hbm.1, bf16[4096,512]{1,0:T(8,128)(2,1)} %centers_hbm.1, f32[32,128]{1,0:T(8,128)} %bitcast.5, s32[1,64]{1,0:T(1,128)} %bitcast.6, ...), custom_call_target="tpu_custom_call" | custom-call | tf_op jit(solution)/shard_map/pallas_call | solution.py:534
  72.0 2.7 %shard_map.94 = (f32[32,128]{1,0:T(8,128)}, bf16[4096,512]{1,0:T(8,128)(2,1)}, f32[64,512]{1,0:T(8,128)}, f32[1,1]{1,0:T(1,128)}) custom-call(f32[32,128]{1,0:T(8,128)S(1)} %get-tuple-element.12.fresh_in, bf16[4096,512]{1,0:T(8,128)(2,1)S(1)} %get-tuple-element.13.cgrad_in, f32[64,512]{1,0:T(8,128)S(1)} %get-tuple-element.14.egrad_in, ...), custom_call_target="tpu_custom_call" | custom-call | tf_op jit(solution)/shard_map/pallas_call | solution.py:547

commit v3 on v2

--- a/solution.py
+++ b/solution.py
@@ -20,6 +20,7 @@
 TCH, TUN = 256, 4
 SCH, SUN = 256, 4
 LANES = 128
+PIECES = 2
 
 
 def unit_rows(values):
@@ -60,6 +61,14 @@
     core = lax.rem(cls, 2)
     plane = lax.div(cls, 2)
     sibling = cls + 1 - 2 * core
+    side = math.isqrt(nplane)
+    x, y = lax.rem(plane, side), lax.div(plane, side)
+    apart = [(dy, dx) for dy in range(side) for dx in range(nplane // side) if dy or dx]
+    apart.sort(key=lambda d: -min(d[0], side - d[0]) - min(d[1], side - d[1]))
+    planes = [lax.rem(y + dy, side) * side + lax.rem(x + dx, side) for dy, dx in apart]
+    z_order = sorted(range(1, nz), key=lambda k: -min(k, nz - k))
+    z_peers = [lax.rem(z + k, nz) for k in z_order]
+    cls_peers = [p * 2 + c for p in planes for c in (core, 1 - core)] + [sibling]
 
     quarter = classes // 4
     own_copies = [
@@ -82,16 +91,11 @@
 
     barrier = pltpu.get_barrier_semaphore()
 
-    def greet_z(k, carry):
-        pl.semaphore_signal(barrier, inc=1, device_id={"dp": lax.rem(z + k, nz)}, device_id_type=MESH)
-        return carry
-
-    def greet_cls(k, carry):
-        pl.semaphore_signal(barrier, inc=1, device_id={"cls": lax.rem(cls + k, ncls)}, device_id_type=MESH)
-        return carry
-
-    lax.fori_loop(1, nz, greet_z, 0)
-    lax.fori_loop(1, ncls, greet_cls, 0)
+    for peer in z_peers:
+        pl.semaphore_signal(barrier, inc=1, device_id={"dp": peer}, device_id_type=MESH)
+    for peer in cls_peers:
+        pl.semaphore_signal(barrier, inc=1, device_id={"cls": peer}, device_id_type=MESH)
+
     base = pl.multiple_of(z * img, img)
     own_copies[0].wait()
     weak_exact, _ = unit_rows(weak_own[...])
@@ -195,31 +199,24 @@
     marginal_columns()
 
     def a_start(n):
-        def go(k, carry):
+        for peer in cls_peers:
             pltpu.make_async_remote_copy(
                 msg_a.at[n], got_a.at[n, cls], a_send.at[n], a_recv.at[n],
-                device_id={"cls": lax.rem(cls + k, ncls)}, device_id_type=MESH,
+                device_id={"cls": peer}, device_id_type=MESH,
             ).start()
-            return carry
-
         got_a[n, cls] = msg_a[n]
-        lax.fori_loop(1, ncls, go, 0)
 
     def b_start(n):
         whole = got_a.at[n, pl.ds(0, ncls - 1)]
         pltpu.make_async_copy(whole, whole, a_recv.at[n]).wait()
         total = jnp.sum(got_a[n], axis=0)
         msg_b[n] = total
-        got_b[n, z] = total
-
-        def go(k, carry):
+        for peer in z_peers:
             pltpu.make_async_remote_copy(
                 msg_b.at[n], got_b.at[n, z], b_send.at[n], b_recv.at[n],
-                device_id={"dp": lax.rem(z + k, nz)}, device_id_type=MESH,
+                device_id={"dp": peer}, device_id_type=MESH,
             ).start()
-            return carry
-
-        lax.fori_loop(1, nz, go, 0)
+        got_b[n, z] = total
 
     def b_finish(n):
         whole = got_b.at[n, pl.ds(0, nz - 1)]
@@ -379,15 +376,11 @@
 
         lax.fori_loop(0, nplane, half_add, 0, unroll=True)
 
-        def plane_copy(k, carry):
-            p = lax.rem(plane + k, nplane)
+        for p in planes:
             pltpu.make_async_remote_copy(
                 half_buf.at[part, core, p], plane_got.at[part, plane], plane_send.at[part], plane_recv.at[part],
                 device_id={"cls": p * 2 + core}, device_id_type=MESH,
             ).start()
-            return carry
-
-        lax.fori_loop(1, nplane, plane_copy, 0)
         plane_got[part, plane] = half_buf[part, core, plane]
 
     for part in range(2):
@@ -427,16 +420,11 @@
             z_send[part * near + block, 0:per] = plane_sum[block * per : (block + 1) * per]
     for block in range(nz):
         z_send[block, per] = plane_sum[last]
-    z_got[z] = z_send[z]
-
-    def z_copy(k, carry):
-        to = lax.rem(z + k, nz)
+    for to in z_peers:
         pltpu.make_async_remote_copy(
             z_send.at[to], z_got.at[z], z_send_sem, z_recv_sem, device_id={"dp": to}, device_id_type=MESH
         ).start()
-        return carry
-
-    lax.fori_loop(1, nz, z_copy, 0)
+    z_got[z] = z_send[z]
 
     two = n_chunks * 7 // 8
     lax.fori_loop(third, two, center_step, 0, unroll=2)
@@ -445,16 +433,12 @@
     pltpu.make_async_copy(whole_z, whole_z, z_recv_sem).wait()
     z_sum = jnp.sum(z_got[...], axis=0)
     tile_own[...] = z_sum[0:per]
+    for peer in cls_peers:
+        pltpu.make_async_remote_copy(
+            tile_own, tile_got.at[cls], tile_send, tile_recv, device_id={"cls": peer}, device_id_type=MESH
+        ).start()
     tile_got[cls] = z_sum[0:per]
 
-    def tile_copy(k, carry):
-        pltpu.make_async_remote_copy(
-            tile_own, tile_got.at[cls], tile_send, tile_recv,
-            device_id={"cls": lax.rem(cls + k, ncls)}, device_id_type=MESH,
-        ).start()
-        return carry
-
-    lax.fori_loop(1, ncls, tile_copy, 0)
     lax.fori_loop(two, n_chunks, center_step, 0, unroll=2)
     loss_rows = flags_block * (SCALE + jnp.log(student_total)) + z_sum[per, 0:blocks, :]
     loss_out[...] = jnp.sum(jnp.sum(loss_rows, axis=1, keepdims=True), axis=0, keepdims=True) / img
@@ -491,7 +475,9 @@
 
 
 def store(fresh_in, cgrad_in, egrad_in, loss_in, fresh_out, cgrad_out, egrad_out, loss_out, sem):
-    parts = ((cgrad_in, cgrad_out), (egrad_in, egrad_out), (fresh_in, fresh_out), (loss_in, loss_out))
+    size = cgrad_in.shape[0] // PIECES
+    parts = [(cgrad_in.at[pl.ds(n * size, size)], cgrad_out.at[pl.ds(n * size, size)]) for n in range(PIECES)]
+    parts += [(egrad_in, egrad_out), (fresh_in, fresh_out), (loss_in, loss_out)]
     copies = [pltpu.make_async_copy(a, b, sem.at[n]) for n, (a, b) in enumerate(parts)]
     for copy in copies:
         copy.start()
@@ -549,7 +535,7 @@
         out_shape=tuple(jax.ShapeDtypeStruct(*shape) for shape in shapes),
         in_specs=[local] * 4,
         out_specs=(hbm,) * 4,
-        scratch_shapes=[dma((4,))],
+        scratch_shapes=[dma((PIECES + 3,))],
         compiler_params=pltpu.CompilerParams(vmem_limit_bytes=1024 * 1024),
     )(*results)
     return fresh.reshape(classes), cgrad, egrad, loss.reshape(())

time: 74.8 us -> 73.5 us (0.983)
  Pallas kernels: 74.1 us -> 72.8 us
    pallas_call x1, Pallas kernels: 71.4 us -> 70 us  [body(): pl.pallas_call(functools.partial(kernel, nz, ncls), out_shape=tuple((pltp...]
where the time goes in v3:
time: 73.5 us; the launch traced here: 73.4 us
  Pallas kernels  72.8 us (99%)
    pallas_call x1, Pallas kernels, body(): pl.pallas_call(functools.partial(kernel, nz, ncls), out_shape=tuple((pltp...  70 us
    pallas_call x1, Pallas kernels, body(): pl.pallas_call(store, out_shape=tuple((jax.ShapeDtypeStruct(*shape) for s...  2.72 us

profile of v3, /device:TPU:1, one launch (start us, length us, event | category | flops | bytes accessed | tf_op | source)
XLA Modules:
  0.0 73.4 jit_solution(12693096711248164686)
XLA Ops:
  0.6 70.0 %shard_map.93 = (f32[32,128]{1,0:T(8,128)S(1)}, bf16[4096,512]{1,0:T(8,128)(2,1)S(1)}, f32[64,512]{1,0:T(8,128)S(1)}, f32[1,1]{1,0:T(1,128)}) custom-call(bf16[64,512]{1,0:T(8,128)(2,1)} %weak_hbm.1, bf16[64,512]{1,0:T(8,128)(2,1)} %strong_hbm.1, bf16[4096,512]{1,0:T(8,128)(2,1)} %centers_hbm.1, f32[32,128]{1,0:T(8,128)} %bitcast.5, s32[1,64]{1,0:T(1,128)} %bitcast.6, ...), custom_call_target="tpu_custom_call" | custom-call | tf_op jit(solution)/shard_map/pallas_call | solution.py:520
  70.7 2.7 %shard_map.94 = (f32[32,128]{1,0:T(8,128)}, bf16[4096,512]{1,0:T(8,128)(2,1)}, f32[64,512]{1,0:T(8,128)}, f32[1,1]{1,0:T(1,128)}) custom-call(f32[32,128]{1,0:T(8,128)S(1)} %get-tuple-element.12.fresh_in, bf16[4096,512]{1,0:T(8,128)(2,1)S(1)} %get-tuple-element.13.cgrad_in, f32[64,512]{1,0:T(8,128)S(1)} %get-tuple-element.14.egrad_in, ...), custom_call_target="tpu_custom_call" | custom-call | tf_op jit(solution)/shard_map/pallas_call | solution.py:533

commit v4 on v3

--- a/solution.py
+++ b/solution.py
@@ -138,8 +138,6 @@
     own_copies[1].wait()
     strong_exact, _ = unit_rows(strong_own[...])
     strong_all[pl.ds(base, img), :] = strong_exact.astype(BF16)
-    for away, k in sends:
-        gather_copy(1, away, k).start()
     own_copies[2].wait()
     own_copies[3].wait()
     mine = ints_own[:, 0:img]
@@ -243,6 +241,9 @@
 
     n_chunks = classes // CH
     zero = jnp.zeros((8, rows), F32)
+
+    for away, k in sends:
+        gather_copy(1, away, k).start()
 
     group_rows = rows // 2
 

time: 73.5 us -> 72.5 us (0.986)
  Pallas kernels: 72.8 us -> 71.8 us
    pallas_call x1, Pallas kernels: 70 us -> 69.1 us  [body(): pl.pallas_call(functools.partial(kernel, nz, ncls), out_shape=tuple((pltp...]
where the time goes in v4:
time: 72.5 us
  Pallas kernels  71.8 us (99%)
    pallas_call x1, Pallas kernels, body(): pl.pallas_call(functools.partial(kernel, nz, ncls), out_shape=tuple((pltp...  69.1 us
    pallas_call x1, Pallas kernels, body(): pl.pallas_call(store, out_shape=tuple((jax.ShapeDtypeStruct(*shape) for s...  2.72 us

profile of v4, /device:TPU:1, one launch (start us, length us, event | category | flops | bytes accessed | tf_op | source)
XLA Modules:
  0.0 72.5 jit_solution(11534068067976639588)
XLA Ops:
  0.6 69.1 %shard_map.93 = (f32[32,128]{1,0:T(8,128)S(1)}, bf16[4096,512]{1,0:T(8,128)(2,1)S(1)}, f32[64,512]{1,0:T(8,128)S(1)}, f32[1,1]{1,0:T(1,128)}) custom-call(bf16[64,512]{1,0:T(8,128)(2,1)} %weak_hbm.1, bf16[64,512]{1,0:T(8,128)(2,1)} %strong_hbm.1, bf16[4096,512]{1,0:T(8,128)(2,1)} %centers_hbm.1, f32[32,128]{1,0:T(8,128)} %bitcast.5, s32[1,64]{1,0:T(1,128)} %bitcast.6, ...), custom_call_target="tpu_custom_call" | custom-call | tf_op jit(solution)/shard_map/pallas_call | solution.py:521
  69.7 2.7 %shard_map.94 = (f32[32,128]{1,0:T(8,128)}, bf16[4096,512]{1,0:T(8,128)(2,1)}, f32[64,512]{1,0:T(8,128)}, f32[1,1]{1,0:T(1,128)}) custom-call(f32[32,128]{1,0:T(8,128)S(1)} %get-tuple-element.12.fresh_in, bf16[4096,512]{1,0:T(8,128)(2,1)S(1)} %get-tuple-element.13.cgrad_in, f32[64,512]{1,0:T(8,128)S(1)} %get-tuple-element.14.egrad_in, ...), custom_call_target="tpu_custom_call" | custom-call | tf_op jit(solution)/shard_map/pallas_call | solution.py:534
